TPU v7x, 512 devices: a whole 4x8x8 slice. The times are simulated.
512 devices in a mesh: dp: 16 (over z_hi, y), tile: 32 (over z_lo, x, core).
Axes of the slice: x: 4, y: 8, z: 8 (z_hi: 2, z_lo: 4; z = z_hi * 4 + z_lo), core: 2. Of those that a mesh axis runs over, the one named last changes fastest.
Arguments:
- activations: bfloat16 [3072, 53248], P('dp', 'tile'), may hold values from -6 to 6
- sign_bits: int32 [53248], P('tile'), may hold values from 0 to 1
- factor_bits: int32 [13], replicated, may hold values from 0 to 1
Outputs:
- gram_slab: float32 [256, 53248], P('dp', 'tile')
All inputs are finite; a program needn't handle non-finite values.
Results may differ from a plain program's by a relative error of at most 0.0083.
Values may be sent and summed in bfloat16 or wider, within the bound.
A program may use at most 128 MiB of HBM per device.

v0:
```python
import jax
import jax.numpy as jnp
from jax import lax
from jax.sharding import PartitionSpec as P

KF = 13
HB = 128
TS = 128
SLAB = 256
HAD = 4096


def swapped(block, axis, stride):
    count = lax.axis_size(axis)
    route = []
    for low in range(count):
        high = low | 1 << stride
        if high != low and high < count:
            route += [(low, high), (high, low)]
    return lax.ppermute(block, axis, route)


def spread_2(shard, axis, root):
    mine = lax.axis_index(axis) == root
    return lax.psum(jnp.where(mine, shard, jnp.zeros_like(shard)), axis)


def sylvester(order):
    index = jnp.arange(order, dtype=jnp.int32)
    both = index[:, None] & index[None, :]
    parity = jnp.zeros((order, order), jnp.int32)
    for shift in range(order.bit_length() - 1):
        parity = parity ^ both >> shift & 1
    return (1 - 2 * parity).astype(jnp.float32)


def local_inner(flipped, factor, width):
    tokens = flipped.shape[0]
    count = flipped.shape[1] // width
    inner = jnp.dot(flipped, factor, preferred_element_type=jnp.float32)
    return inner.reshape(tokens, count, width)


def spread_bits(field):
    position = lax.axis_index("tile")
    for level in range(lax.axis_size("tile").bit_length() - 1):
        partner = swapped(field, "tile", level)
        upper = position >> level & 1 == 1
        field = jnp.where(upper, partner - field, field + partner)
    return field


def shards(activations, sign_bits, factor_bits):
    width = HB * KF
    scale = 1.0 / float(HAD) ** 0.5
    tok_rows = activations.shape[0]
    cols_dev = activations.shape[1]
    flipped = activations * (1 - 2 * sign_bits).astype(jnp.bfloat16)[None, :]
    vector = (1 - 2 * factor_bits).astype(jnp.float32)
    reflect = jnp.eye(KF, dtype=jnp.float32) - 2.0 / KF * vector[:, None] * vector[None, :]
    hblock = sylvester(HB)
    factor = (
        (hblock[:, None, :, None] * reflect[None, :, None, :])
        .reshape(width, width)
        .astype(jnp.bfloat16)
    )
    inner = local_inner(flipped, factor, width)
    hgroup = sylvester(inner.shape[1])
    mixed = jnp.einsum("kl,tlc->tkc", hgroup, inner, precision=lax.Precision.HIGHEST)
    spread = spread_bits(mixed.reshape(tok_rows, cols_dev))
    rotated = (spread * scale).astype(jnp.bfloat16)
    slab = spread_2(rotated[:, :SLAB], "tile", 0)
    first_col = lax.axis_index("tile") * cols_dev
    col_tile = (first_col + jnp.arange(cols_dev, dtype=jnp.int32)) // TS
    part = jnp.einsum("tr,tc->rc", slab, rotated, preferred_element_type=jnp.float32)
    row_tile = jnp.arange(SLAB // lax.axis_size("dp") * lax.axis_size("dp"), dtype=jnp.int32) // TS
    keep = col_tile[None, :] >= row_tile[:, None]
    summed = lax.psum_scatter(jnp.where(keep, part, 0.0), "dp", scatter_dimension=0, tiled=True)
    total_tokens = tok_rows * lax.axis_size("dp")
    return summed * (2.0 / total_tokens)


def solution(mesh):
    return jax.shard_map(
        shards,
        mesh=mesh,
        in_specs=(P("dp", "tile"), P("tile"), P()),
        out_specs=P("dp", "tile"),
        check_vma=False,
    )
```

profile of v0, /device:TPU:6, one launch (start us, length us, event | category | flops | bytes accessed | tf_op | source)
XLA Modules:
  0.0 760.0 jit_solution(12042207153063306542)
XLA Ops:
  6.5 0.7 subtract_convert_fusion.2
  7.2 0.7 broadcast_multiply_fusion.1
  8.0 17.7 %multiply_convert_fusion = bf16[128,13,128,13]{3,2,1,0:T(8,128)(2,1)} fusion(f32[13,13]{1,0:T(8,128)S(1)} %multiply_subtract_fusion, f32[128,128]{1,0:T(8,128)S(1)} %subtract_convert_fusion), kind=kLoop, calls=%fused_computation | loop fusion | flops 5537792 | bytes 5604004 | tf_op jit(solution)/shard_map/convert_element_type | solution.py:65
  25.7 64.9 %convert_element_type.34 = bf16[1664,1664]{1,0:T(8,128)(2,1)} reshape(bf16[128,13,128,13]{3,2,1,0:T(8,128)(2,1)} %multiply_convert_fusion) | data formatting | bytes 11075584 | tf_op jit(solution)/shard_map/convert_element_type | solution.py:65
  90.7 4.0 fusion
  94.6 1.9 collective-permute-start
  96.6 3.1 collective-permute-done
  99.7 1.4 add_select_fusion.3
  101.1 2.7 collective-permute-start.1
  103.9 29.4 %collective-permute-done.1 = f32[192,1664]{1,0:T(8,128)} collective-permute-done((f32[192,1664]{1,0:T(8,128)S(1)}, f32[192,1664]{1,0:T(8,128)}, u32[]{:S(2)}, u32[]{:S(2)}) %collective-permute-start.1) | collective-permute-done | bytes 1277984 | tf_op jit(solution)/shard_map/ppermute | solution.py:20
  133.2 1.4 add_select_fusion.2
  134.7 7.5 collective-permute-start.2
  142.2 28.0 %collective-permute-done.2 = f32[192,1664]{1,0:T(8,128)} collective-permute-done((f32[192,1664]{1,0:T(8,128)S(1)}, f32[192,1664]{1,0:T(8,128)}, u32[]{:S(2)}, u32[]{:S(2)}) %collective-permute-start.2) | collective-permute-done | bytes 1277984 | tf_op jit(solution)/shard_map/ppermute | solution.py:20
  170.1 1.4 add_select_fusion.1
  171.6 1.9 collective-permute-start.3
  173.5 29.1 %collective-permute-done.3 = f32[192,1664]{1,0:T(8,128)} collective-permute-done((f32[192,1664]{1,0:T(8,128)S(1)}, f32[192,1664]{1,0:T(8,128)}, u32[]{:S(2)}, u32[]{:S(2)}) %collective-permute-start.3) | collective-permute-done | bytes 1277984 | tf_op jit(solution)/shard_map/ppermute | solution.py:20
  202.6 1.4 add_select_fusion
  204.0 3.4 collective-permute-start.4
  207.5 54.8 %collective-permute-done.4 = f32[192,1664]{1,0:T(8,128)S(1)} collective-permute-done((f32[192,1664]{1,0:T(8,128)S(1)}, f32[192,1664]{1,0:T(8,128)S(1)}, u32[]{:S(2)}, u32[]{:S(2)}) %collective-permute-start.4) | collective-permute-done | bytes 1277984 | tf_op jit(solution)/shard_map/ppermute | solution.py:20
  262.5 0.7 slice_select_fusion
  263.2 246.3 %all-reduce.2.cloned.1.call-done = bf16[192,256]{1,0:T(8,128)(2,1)} async-done(((bf16[192,256]{1,0:T(8,128)(2,1)}), bf16[192,256]{1,0:T(8,128)(2,1)}) %all-reduce.2.cloned.1.call-update) | async-done | bytes 98320 | tf_op jit(solution)/shard_map/psum | solution.py:25
  509.5 2.5 convolution_select_fusion
  512.1 239.5 %reduce-scatter.2.cloned.1.call-done = f32[16,1664]{1,0:T(8,128)} async-done(((f32[256,1664]{1,0:T(8,128)}), f32[16,1664]{1,0:T(8,128)}) %reduce-scatter.2.cloned.1.call-update) | async-done | bytes 106512 | tf_op jit(solution)/shard_map/reduce_scatter | solution.py:78
  751.6 1.5 broadcast_multiply_fusion
  (14 shorter events, 0.4 us)
Async XLA Ops:
  6.5 503.0 %all-reduce.2.cloned.1.call-start = ((), (), s32[]{:S(2)}) async-start(), calls=%async_computation.1 | async-start | bytes 196608 | tf_op jit(solution)/shard_map/psum | solution.py:25
  25.7 64.9 %copy-start.1 = (s32[1664]{0:T(1024)S(1)}, s32[1664]{0:T(1024)}, u32[]{:S(2)}) copy-start(s32[1664]{0:T(1024)} %param.4) | copy-start | bytes 19972
  25.7 65.0 %copy-start = (bf16[192,1664]{1,0:T(8,128)(2,1)S(1)}, bf16[192,1664]{1,0:T(8,128)(2,1)}, u32[]{:S(2)}) copy-start(bf16[192,1664]{1,0:T(8,128)(2,1)} %param.3) | copy-start | bytes 1916932
  94.6 5.0 collective-permute-start
  101.1 32.1 %collective-permute-start.1 = (f32[192,1664]{1,0:T(8,128)S(1)}, f32[192,1664]{1,0:T(8,128)}, u32[]{:S(2)}, u32[]{:S(2)}) collective-permute-start(f32[192,1664]{1,0:T(8,128)S(1)} %add_select_fusion.3), channel_id=1, source_target_pairs={{0,2},{2,0},{1,3},{3,1},{4,6},{6,4},{5,7},{7,5},{8,10},{10,8},{9,1... | collective-permute-start | bytes 3833864 | tf_op jit(solution)/shard_map/ppermute | solution.py:20
  134.7 35.5 %collective-permute-start.2 = (f32[192,1664]{1,0:T(8,128)S(1)}, f32[192,1664]{1,0:T(8,128)}, u32[]{:S(2)}, u32[]{:S(2)}) collective-permute-start(f32[192,1664]{1,0:T(8,128)S(1)} %add_select_fusion.2), channel_id=1, source_target_pairs={{0,4},{4,0},{1,5},{5,1},{2,6},{6,2},{3,7},{7,3},{8,12},{12,8},{9,1... | collective-permute-start | bytes 3833864 | tf_op jit(solution)/shard_map/ppermute | solution.py:20
  171.6 31.0 %collective-permute-start.3 = (f32[192,1664]{1,0:T(8,128)S(1)}, f32[192,1664]{1,0:T(8,128)}, u32[]{:S(2)}, u32[]{:S(2)}) collective-permute-start(f32[192,1664]{1,0:T(8,128)S(1)} %add_select_fusion.1), channel_id=1, source_target_pairs={{0,8},{8,0},{1,9},{9,1},{2,10},{10,2},{3,11},{11,3},{4,12},{12,4},... | collective-permute-start | bytes 3833864 | tf_op jit(solution)/shard_map/ppermute | solution.py:20
  204.0 58.3 %collective-permute-start.4 = (f32[192,1664]{1,0:T(8,128)S(1)}, f32[192,1664]{1,0:T(8,128)S(1)}, u32[]{:S(2)}, u32[]{:S(2)}) collective-permute-start(f32[192,1664]{1,0:T(8,128)S(1)} %add_select_fusion), channel_id=1, source_target_pairs={{0,16},{16,0},{1,17},{17,1},{2,18},{18,2},{3,19},{19,3},{4,20},{20... | collective-permute-start | bytes 3833864 | tf_op jit(solution)/shard_map/ppermute | solution.py:20
  263.2 488.4 %reduce-scatter.2.cloned.1.call-start = ((), (), s32[]{:S(2)}) async-start(), calls=%async_computation.2 | async-start | bytes 1810432 | tf_op jit(solution)/shard_map/reduce_scatter | solution.py:78
Sparse Core Ops, SparseCore 0:
  263.3 246.1 all-reduce.1
  514.7 236.8 reduce-scatter.1
where the time goes:
time: 762 us; the launch traced here: 760 us
  waiting for transfers between devices  630 us (83%)
  local copies, waits for them, and re-layouts  64.9 us (9%)
  other arithmetic  27.3 us (4%)
  starting transfers between devices  17.5 us (2%)
  between operations  13.5 us (2%)
    psum x1, waiting for transfers between devices, spread_2(): return lax.psum(jnp.where(mine, shard, jnp.zeros_like(shard)), axis)  246 us
    reduce_scatter x1, waiting for transfers between devices, shards(): lax.psum_scatter(jnp.where(keep, part, 0.0), 'dp', scatter_dimension=0, t...  240 us
    ppermute x5, waiting for transfers between devices, swapped(): return lax.ppermute(block, axis, route)  144 us
    convert_element_type x1, local copies, waits for them, and re-layouts, shards(): factor = (hblock[:, None, :, None] * reflect[None, :, None, :]).reshape(w...  64.9 us
    convert_element_type x1, other arithmetic, shards(): factor = (hblock[:, None, :, None] * reflect[None, :, None, :]).reshape(w...  17.7 us
    ppermute x5, starting transfers between devices, swapped(): return lax.ppermute(block, axis, route)  17.5 us
  transfers between devices with their start and end apart: 7, of which 7 were waited for; matrix products, arithmetic and copies ran while one was open for 0% of the time, Pallas kernels for 0%

commit v1 on v0

v1 whole, which is shorter than its diff:
```python
import functools

import jax
import jax.numpy as jnp
import ml_dtypes
import numpy as np
from jax import lax
from jax.experimental import pallas as pl
from jax.experimental.pallas import tpu as pltpu
from jax.sharding import PartitionSpec as P

KF = 13
HB = 128
WIDTH = KF * HB
SLAB = 256
HAD = 4096
LANES = 128
NT = WIDTH // LANES
MESH = pl.DeviceIdType.MESH
BF = jnp.bfloat16
F32 = jnp.float32


def small_factor():
    index = np.arange(HB)
    both = index[:, None] & index[None, :]
    parity = np.zeros_like(both)
    for shift in range(7):
        parity ^= (both >> shift) & 1
    hblock = (1 - 2 * parity).astype(np.float32)
    refl = np.eye(KF, dtype=np.float32) - np.float32(2.0 / KF)
    return np.kron(hblock, refl).astype(ml_dtypes.bfloat16)


def butterfly(parts):
    step = 1
    parts = list(parts)
    while step < len(parts):
        for low in range(len(parts)):
            if not low & step:
                a, b = parts[low], parts[low | step]
                parts[low], parts[low | step] = a + b, a - b
        step *= 2
    return parts


def parity_sign(mine, other, bits):
    total = 0
    for bit in range(bits):
        if other >> bit & 1:
            total = total + mine // (1 << bit) % 2
    return (1 - 2 * (total % 2)).astype(F32) if not isinstance(total, int) else None


def kernel(
    dims,
    act_hbm, sign_ref, bits_ref, fac_hbm,
    out_ref,
    x_buf, fac_buf, inner, ysend, yrecv, ymid, yzrecv, yfull,
    gp, rs, pbuf, zbuf, zlast, ubuf, xbuf, wbuf, obuf,
    load_sem, y1s, y1r, y2s, y2r, y3s, y3r, rss, rsr, zs, zr, xs_s, xs_r, as_s, as_r,
):
    ny, nzl, nx, nc = dims
    nxc = nx * nc
    rows = SLAB // (2 * ny)
    tokens = act_hbm.shape[0]
    piece = tokens // nx
    nch = NT // nzl
    dp, tile = lax.axis_index("dp"), lax.axis_index("tile")
    zh, y = dp // ny, dp % ny
    zl, xc = tile // nxc, tile % nxc

    def at(zh_, y_, zl_, xc_):
        return (zh_ * ny + y_, zl_ * nxc + xc_)

    def xc_peer(k):
        return at(zh, y, zl, (xc + k) % nxc)

    def z_peer(a, k):
        return at((zh + a) % 2, y, (zl + k) % nzl, xc)

    z_moves = [(a, k) for a in range(2) for k in range(nzl) if (a, k) != (0, 0)]

    def remote(src, dst, send, recv, peer):
        copy = pltpu.make_async_remote_copy(
            src_ref=src, dst_ref=dst, send_sem=send, recv_sem=recv, device_id=peer, device_id_type=MESH
        )
        copy.start()
        return copy

    load_x = pltpu.make_async_copy(act_hbm, x_buf, load_sem.at[0])
    load_a = pltpu.make_async_copy(fac_hbm.at[:, pl.ds(0, SLAB)], fac_buf.at[:, pl.ds(0, SLAB)], load_sem.at[1])
    load_b = pltpu.make_async_copy(
        fac_hbm.at[:, pl.ds(SLAB, WIDTH - SLAB)], fac_buf.at[:, pl.ds(SLAB, WIDTH - SLAB)], load_sem.at[2]
    )
    load_x.start()
    load_a.start()
    load_b.start()

    barrier = pltpu.get_barrier_semaphore()
    peers = [xc_peer(k) for k in range(1, nxc)] + [z_peer(a, k) for a, k in z_moves]
    peers += [at(zh, (y + 1) % ny, zl, xc), at(zh, (y + ny - 1) % ny, zl, xc)]
    for peer in peers:
        pl.semaphore_signal(barrier, inc=1, device_id=peer, device_id_type=MESH)

    col = lax.broadcasted_iota(jnp.int32, (1, WIDTH), 1)
    b_of = col - KF * ((col * 20165) >> 18)
    vee = jnp.zeros((1, WIDTH), F32)
    for b in range(KF):
        vee = jnp.where(b_of == b, (1 - 2 * bits_ref[b]).astype(F32), vee)
    flip = ((1 - 2 * sign_ref[...]).astype(F32) * vee).astype(BF)

    load_x.wait()
    x_buf[...] = x_buf[...] * flip
    load_a.wait()

    part = jnp.dot(x_buf[...], fac_buf[:, :SLAB], preferred_element_type=F32) * vee[:, :SLAB]
    inner[:, :SLAB] = part.astype(BF)
    for ix in range(nx):
        for ic in range(2):
            ysend[ix * 2 + ic] = part[ix * piece:(ix + 1) * piece, ic * LANES:(ic + 1) * LANES].astype(BF)
    pl.semaphore_wait(barrier, len(peers))

    def more_inner(first, last):
        for c0 in range(first, last, 256):
            c1 = min(c0 + 256, last)
            got = jnp.dot(x_buf[...], fac_buf[:, c0:c1], preferred_element_type=F32) * vee[:, c0:c1]
            inner[:, c0:c1] = got.astype(BF)

    moves = [
        remote(ysend.at[(xc + k) % nxc], yrecv.at[k], y1s.at[k], y1r.at[k], xc_peer(k)) for k in range(1, nxc)
    ]
    load_b.wait()
    more_inner(256, 768)
    total = ysend[xc].astype(F32)
    for k in range(1, nxc):
        moves[k - 1].wait_recv()
        total = total + yrecv[k].astype(F32)
    ymid[...] = total.astype(BF)
    moves2 = [
        remote(ymid, yzrecv.at[k], y2s.at[k], y2r.at[k], z_peer(0, k)) for k in range(1, nzl)
    ]
    more_inner(768, 1280)
    total = ymid[...].astype(F32)
    for k in range(1, nzl):
        moves2[k - 1].wait_recv()
        total = total + yzrecv[k].astype(F32)
    yfull[xc] = total.astype(BF)
    moves3 = [
        remote(yfull.at[xc], yfull.at[xc], y3s.at[k], y3r.at[k], xc_peer(k)) for k in range(1, nxc)
    ]
    more_inner(1280, WIDTH)
    for move in moves3:
        move.wait_recv()

    for half in range(2):
        left = jnp.concatenate([yfull[ix * 2 + half] for ix in range(nx)], axis=0)
        for c0 in range(0, WIDTH, 256):
            c1 = min(c0 + 256, WIDTH)
            got = lax.dot_general(
                left, inner[:, c0:c1], (((0,), (0,)), ((), ())), preferred_element_type=F32
            ).astype(BF)
            for iy in range(ny):
                for j in range((c1 - c0) // LANES):
                    gp[iy, half, c0 // LANES + j] = got[iy * rows:(iy + 1) * rows, j * LANES:(j + 1) * LANES]

    chunks = [(nzl * m, nzl * m + nzl if m < nch - 1 else NT) for m in range(nch)]
    top = ny // 2
    ways = [(way, half) for way in range(2) for half in range(2)]
    rs_moves = {}

    def far(way, half):
        return top if way == half else top - 1

    def rs_send(src, way, half, dist, m):
        lo, hi = chunks[m]
        step = 1 if way == 0 else ny - 1
        index = ((way * 2 + half) * top + dist - 1) * nch + m
        rs_moves[way, half, dist, m] = remote(
            src, rs.at[way, half, dist - 1, pl.ds(lo, hi - lo)], rss.at[index], rsr.at[index],
            at(zh, (y + step) % ny, zl, xc),
        )

    def owner(way, dist):
        return (y + dist) % ny if way == 0 else (y + ny - dist) % ny

    for m in range(nch):
        lo, hi = chunks[m]
        for way, half in ways:
            dist = far(way, half)
            if dist == top:
                rs_send(gp.at[owner(way, dist), half, pl.ds(lo, hi - lo)], way, half, dist, m)
        for way, half in ways:
            dist = far(way, half)
            if 0 < dist < top:
                rs_send(gp.at[owner(way, dist), half, pl.ds(lo, hi - lo)], way, half, dist, m)
    for dist in range(top - 1, 0, -1):
        for m in range(nch):
            lo, hi = chunks[m]
            for way, half in ways:
                if dist < far(way, half):
                    rs_moves[way, half, dist + 1, m].wait_recv()
                    slot = rs.at[way, half, dist, pl.ds(lo, hi - lo)]
                    slot[...] = (
                        slot[...].astype(F32) + gp[owner(way, dist), half, pl.ds(lo, hi - lo)].astype(F32)
                    ).astype(BF)
                    rs_send(slot, way, half, dist, m)

    z_copies, x_copies, a_copies = {}, {}, {}
    for m in range(nch):
        lo, hi = chunks[m]
        for half in range(2):
            total = gp[y, half, pl.ds(lo, hi - lo)].astype(F32)
            for way in range(2):
                if (way, half, 1, m) in rs_moves:
                    rs_moves[way, half, 1, m].wait_recv()
                    total = total + rs[way, half, 0, pl.ds(lo, hi - lo)].astype(F32)
            pbuf[half, pl.ds(lo, hi - lo)] = total.astype(BF)
        for n, (a, k) in enumerate(z_moves):
            index = m * len(z_moves) + n
            z_copies[m, n] = remote(
                pbuf.at[(zh + a) % 2, lo + (zl + k) % nzl], zbuf.at[m, zh, zl], zs.at[index], zr.at[index], z_peer(a, k)
            )
        zbuf[m, zh, zl] = pbuf[zh, lo + zl]
        if hi - lo > nzl:
            for n, (a, k) in enumerate(z_moves):
                index = nch * len(z_moves) + n
                z_copies[nch, n] = remote(
                    pbuf.at[(zh + a) % 2, NT - 1], zlast.at[zh, zl], zs.at[index], zr.at[index], z_peer(a, k)
                )
            zlast[zh, zl] = pbuf[zh, NT - 1]

    zbits = nzl.bit_length() - 1
    xbits = nxc.bit_length() - 1

    def mix(parts, mine, bits):
        total = None
        for j, value in enumerate(parts):
            sign = parity_sign(mine, j, bits)
            value = value if sign is None else value * sign
            total = value if total is None else total + value
        return total

    for m in range(nch):
        lo, hi = chunks[m]
        count = hi - lo
        for n in range(len(z_moves)):
            z_copies[m, n].wait_recv()
        mixed = butterfly([zbuf[m, 0, l].astype(F32) + zbuf[m, 1, l].astype(F32) for l in range(nzl)])
        for kz in range(nzl):
            ubuf[lo + kz] = mixed[kz].astype(BF)
        if count > nzl:
            for n in range(len(z_moves)):
                z_copies[nch, n].wait_recv()
            ubuf[NT - 1] = mix(
                [zlast[0, l].astype(F32) + zlast[1, l].astype(F32) for l in range(nzl)], zl, zbits
            ).astype(BF)
        for k in range(1, nxc):
            index = m * nxc + k
            x_copies[m, k] = remote(
                ubuf.at[pl.ds(lo, count)], xbuf.at[xc, pl.ds(lo, count)], xs_s.at[index], xs_r.at[index], xc_peer(k)
            )
        xbuf[xc, pl.ds(lo, count)] = ubuf[pl.ds(lo, count)]

    for m in range(nch):
        lo, hi = chunks[m]
        count = hi - lo
        for k in range(1, nxc):
            x_copies[m, k].wait_recv()
        full = mix([xbuf[j, pl.ds(lo, count)].astype(F32) for j in range(nxc)], xc, xbits)
        wbuf[pl.ds(lo, count)] = full.astype(BF)
        for k in range(1, nzl):
            index = m * nzl + k
            a_copies[m, k] = remote(
                wbuf.at[lo + (zl + k) % nzl], obuf.at[lo + zl], as_s.at[index], as_r.at[index], z_peer(0, k)
            )
        obuf[lo + zl] = wbuf[lo + zl]
        if count > nzl:
            out_ref[:, (NT - 1) * LANES:] = full[count - 1]

    for m in range(nch):
        lo, hi = chunks[m]
        for k in range(1, nzl):
            a_copies[m, k].wait_recv()
        for j in range(nzl):
            out_ref[:, (lo + j) * LANES:(lo + j + 1) * LANES] = obuf[lo + j].astype(F32)

    for group in (moves, moves2, moves3, rs_moves.values(), z_copies.values(), x_copies.values(), a_copies.values()):
        for move in group:
            move.wait_send()


def shards(dims, activations, sign_bits, factor_bits):
    ny, nzl, nx, nc = dims
    nxc = nx * nc
    rows = SLAB // (2 * ny)
    tokens = activations.shape[0]
    piece = tokens // nx
    nch = NT // nzl
    top = ny // 2
    dma = pltpu.SemaphoreType.DMA
    vm = pltpu.VMEM
    n_rs = 4 * top * nch
    n_z = (nch + 1) * (2 * nzl - 1)
    n_x = nch * nxc
    n_a = nch * nzl
    gram = pl.pallas_call(
        functools.partial(kernel, dims),
        out_shape=jax.ShapeDtypeStruct((rows, WIDTH), F32),
        in_specs=[
            pl.BlockSpec(memory_space=pl.ANY),
            pl.BlockSpec(memory_space=pltpu.VMEM),
            pl.BlockSpec(memory_space=pltpu.SMEM),
            pl.BlockSpec(memory_space=pl.ANY),
        ],
        out_specs=pl.BlockSpec(memory_space=pltpu.VMEM),
        scratch_shapes=[
            vm((tokens, WIDTH), BF),
            vm((WIDTH, WIDTH), BF),
            vm((tokens, WIDTH), BF),
            vm((nxc, piece, LANES), BF),
            vm((nxc, piece, LANES), BF),
            vm((piece, LANES), BF),
            vm((nzl, piece, LANES), BF),
            vm((nxc, piece, LANES), BF),
            vm((ny, 2, NT, rows, LANES), BF),
            vm((2, 2, top, NT, rows, LANES), BF),
            vm((2, NT, rows, LANES), BF),
            vm((nch, 2, nzl, rows, LANES), BF),
            vm((2, nzl, rows, LANES), BF),
            vm((NT, rows, LANES), BF),
            vm((nxc, NT, rows, LANES), BF),
            vm((NT, rows, LANES), BF),
            vm((NT, rows, LANES), BF),
            dma((3,)),
            dma((nxc,)), dma((nxc,)),
            dma((nzl,)), dma((nzl,)),
            dma((nxc,)), dma((nxc,)),
            dma((n_rs,)), dma((n_rs,)),
            dma((n_z,)), dma((n_z,)),
            dma((n_x,)), dma((n_x,)),
            dma((n_a,)), dma((n_a,)),
        ],
        compiler_params=pltpu.CompilerParams(
            collective_id=0, has_side_effects=True, vmem_limit_bytes=40 * 1024 * 1024
        ),
    )(activations, sign_bits.reshape(1, WIDTH), factor_bits, jnp.asarray(small_factor()))
    row = lax.axis_index("dp") * rows + lax.broadcasted_iota(jnp.int32, gram.shape, 0)
    col = lax.axis_index("tile") * WIDTH + lax.broadcasted_iota(jnp.int32, gram.shape, 1)
    keep = col // LANES >= row // LANES
    all_tokens = tokens * 2 * ny
    return jnp.where(keep, gram * (2.0 / all_tokens / HAD), 0.0)


def solution(mesh, dims=(8, 4, 4, 2)):
    return jax.shard_map(
        functools.partial(shards, dims),
        mesh=mesh,
        in_specs=(P("dp", "tile"), P("tile"), P()),
        out_specs=P("dp", "tile"),
        check_vma=False,
    )
```

time: 762 us -> 62.4 us (0.08)
  the two profiles are of different devices: /device:TPU:6 before, /device:TPU:1 now
where the time goes in v1:
time: 62.4 us; the launch traced here: 62.2 us
  Pallas kernels  56.4 us (90%)
  local copies, waits for them, and re-layouts  5.01 us (8%)
  other arithmetic  0.77 us (1%)
    pallas_call x1, Pallas kernels, shards(): pl.pallas_call(functools.partial(kernel, dims), out_shape=jax.ShapeDtypeS...  56.4 us
    unnamed x6, local copies, waits for them, and re-layouts  4.31 us

profile of v1, /device:TPU:1, one launch (start us, length us, event | category | flops | bytes accessed | tf_op | source)
XLA Modules:
  0.0 62.2 jit_solution(16072451005328034373)
XLA Ops:
  0.0 0.7 %reshape.3.sign_ref = s32[1,1664]{1,0:T(1,128)S(1)} reshape(s32[1664]{0:T(1024)} %param.5) | data formatting | bytes 13312 | tf_op jit(solution)/shard_map/reshape | solution.py:347
  0.7 0.0 copy-start
  0.7 2.6 %copy-done = bf16[1664,1664]{1,0:T(8,128)(2,1)S(1)} copy-done((bf16[1664,1664]{1,0:T(8,128)(2,1)S(1)}, bf16[1664,1664]{1,0:T(8,128)(2,1)}, u32[]{:S(2)}) %copy-start) | copy-done | bytes 5537816
  3.3 0.0 copy-start.1
  3.3 1.1 %copy-done.1 = bf16[192,1664]{1,0:T(8,128)(2,1)S(1)} copy-done((bf16[192,1664]{1,0:T(8,128)(2,1)S(1)}, bf16[192,1664]{1,0:T(8,128)(2,1)}, u32[]{:S(2)}) %copy-start.1) | copy-done | bytes 639000
  4.4 0.0 copy-start.2
  4.4 0.7 %copy-done.2 = s32[13]{0:T(128)S(1)} copy-done((s32[13]{0:T(128)S(1)}, s32[13]{0:T(128)}, u32[]{:S(2)}) %copy-start.2) | copy-done | bytes 76
  5.0 56.4 %shard_map.46 = f32[16,1664]{1,0:T(8,128)S(1)} custom-call(bf16[192,1664]{1,0:T(8,128)(2,1)S(1)} %copy-done.1, s32[1,1664]{1,0:T(1,128)S(1)} %reshape.3.sign_ref, s32[13]{0:T(128)S(1)} %copy-done.2, bf16[1664,1664]{1,0:T(8,128)(2,1)S(1)} %copy-done), custom_call_target="tpu_custom_call" | custom-call | tf_op jit(solution)/shard_map/pallas_call | solution.py:307
  61.5 0.7 %multiply_select_fusion = f32[16,1664]{1,0:T(8,128)} fusion(f32[16,1664]{1,0:T(8,128)S(1)} %shard_map.46, s32[16]{0:T(128)S(1)} %get-tuple-element.5, s32[16]{0:T(128)S(1)} %get-tuple-element.6, s32[1664]{0:T(1024)S(1)} %get-tuple-element.7, s32[1664]{0:T(1024)S(1)} %get-tuple-element.8, pred[16]{0:T(512)(128)(4,1)S(1)} %compare_and_fusion, ...), kind=kLoop, calls=%fused_computation | loop fusion | flops 133120 | bytes 228112 | tf_op jit(solution)/shard_map/jit(_where)/select_n | solution.py:352
  (4 shorter events, 0.0 us)
Async XLA Ops:
  0.7 2.6 %copy-start = (bf16[1664,1664]{1,0:T(8,128)(2,1)S(1)}, bf16[1664,1664]{1,0:T(8,128)(2,1)}, u32[]{:S(2)}) copy-start(bf16[1664,1664]{1,0:T(8,128)(2,1)} %constant.50.clone.fac_hbm) | copy-start | bytes 16613380
  3.3 1.1 %copy-start.1 = (bf16[192,1664]{1,0:T(8,128)(2,1)S(1)}, bf16[192,1664]{1,0:T(8,128)(2,1)}, u32[]{:S(2)}) copy-start(bf16[192,1664]{1,0:T(8,128)(2,1)} %act_hbm.1) | copy-start | bytes 1916932
  4.4 0.7 %copy-start.2 = (s32[13]{0:T(128)S(1)}, s32[13]{0:T(128)}, u32[]{:S(2)}) copy-start(s32[13]{0:T(128)} %bits_ref.1) | copy-start | bytes 160

commit v2 on v1

v2 whole, which is shorter than its diff:
```python
import functools

import jax
import jax.numpy as jnp
import ml_dtypes
import numpy as np
from jax import lax
from jax.experimental import pallas as pl
from jax.experimental.pallas import tpu as pltpu
from jax.sharding import PartitionSpec as P

KF = 13
HB = 128
WIDTH = KF * HB
SLAB = 256
HAD = 4096
LANES = 128
NT = WIDTH // LANES
CHUNKS = 3
VMEM_LIMIT = 60 * 1024 * 1024
MESH = pl.DeviceIdType.MESH
BF = jnp.bfloat16
F32 = jnp.float32


def small_factor():
    index = np.arange(HB)
    both = index[:, None] & index[None, :]
    parity = np.zeros_like(both)
    for shift in range(7):
        parity ^= (both >> shift) & 1
    hblock = (1 - 2 * parity).astype(np.float32)
    refl = np.eye(KF, dtype=np.float32) - np.float32(2.0 / KF)
    return np.kron(hblock, refl).astype(ml_dtypes.bfloat16)


def butterfly(parts):
    step = 1
    parts = list(parts)
    while step < len(parts):
        for low in range(len(parts)):
            if not low & step:
                a, b = parts[low], parts[low | step]
                parts[low], parts[low | step] = a + b, a - b
        step *= 2
    return parts


def kernel(
    dims,
    act_hbm, sign_ref, bits_hbm, fac_hbm,
    out_ref,
    x_buf, fac_buf, inner, other, bits_ref, ysend, yrecv, ymid, yzrecv, yfull,
    gp, rs_agg, rs_half, rs_near, rs_two, agg, pbuf, mbuf, wbuf, obuf,
    load_sem, core_sem, y1s, y1r, y2s, y2r, y3s, y3r, rss, rsr, ms, mr, bs, br, group_sem,
):
    ny, nzl, nx, nc = dims
    nxc = nx * nc
    nq = nzl * nx
    rows = SLAB // (2 * ny)
    tokens = act_hbm.shape[0]
    piece = tokens // nx
    dp, tile = lax.axis_index("dp"), lax.axis_index("tile")
    zh, y = dp // ny, dp % ny
    zl, xc = tile // nxc, tile % nxc
    x, core = xc // nc, xc % nc
    q = zl * nx + x
    sent = []

    def at(zh_, y_, zl_, xc_):
        return (zh_ * ny + y_, zl_ * nxc + xc_)

    def xc_peer(k):
        return at(zh, y, zl, (xc + k) % nxc)

    def z_peer(k):
        return at(zh, y, (zl + k) % nzl, xc)

    def y_peer(k):
        return at(zh, (y + k + ny) % ny, zl, xc)

    def q_peer(a, k):
        far = (q + k) % nq
        return at((zh + a) % 2, y, far // nx, far % nx * nc + core)

    def remote(src, dst, send, recv, peer):
        copy = pltpu.make_async_remote_copy(
            src_ref=src, dst_ref=dst, send_sem=send, recv_sem=recv, device_id=peer, device_id_type=MESH
        )
        copy.start()
        return copy

    def kept(*args):
        sent.append(remote(*args))
        return sent[-1]

    load_bits = pltpu.make_async_copy(bits_hbm, bits_ref, load_sem.at[3])
    load_x = pltpu.make_async_copy(act_hbm, x_buf, load_sem.at[0])
    load_a = pltpu.make_async_copy(fac_hbm.at[:, pl.ds(0, SLAB)], fac_buf.at[:, pl.ds(0, SLAB)], load_sem.at[1])
    load_b = pltpu.make_async_copy(
        fac_hbm.at[:, pl.ds(SLAB, WIDTH - SLAB)], fac_buf.at[:, pl.ds(SLAB, WIDTH - SLAB)], load_sem.at[2]
    )
    load_bits.start()
    load_x.start()
    load_a.start()
    load_b.start()

    barrier = pltpu.get_barrier_semaphore()
    peers = [xc_peer(k) for k in range(1, nxc)] + [z_peer(k) for k in range(1, nzl)]
    peers += [y_peer(k) for k in (1, -1, 2, -2)]
    for peer in peers:
        pl.semaphore_signal(barrier, inc=1, device_id=peer, device_id_type=MESH)

    @pl.when(zl == 0)
    def _():
        pl.semaphore_signal(barrier, inc=1, device_id=at(1 - zh, y, nzl - 1, xc), device_id_type=MESH)

    col = lax.broadcasted_iota(jnp.int32, (1, WIDTH), 1)
    b_of = col - KF * ((col * 20165) >> 18)
    load_bits.wait()
    vee = jnp.zeros((1, WIDTH), F32)
    for b in range(KF):
        vee = jnp.where(b_of == b, (1 - 2 * bits_ref[b]).astype(F32), vee)
    flip = ((1 - 2 * sign_ref[...].reshape(1, WIDTH)).astype(F32) * vee).astype(BF)

    load_x.wait()
    x_buf[...] = x_buf[...] * flip
    load_a.wait()

    part = jnp.dot(x_buf[...], fac_buf[:, :SLAB], preferred_element_type=F32) * vee[:, :SLAB]
    inner[:, :SLAB] = part.astype(BF)
    for ix in range(nx):
        for ic in range(2):
            ysend[ix * 2 + ic] = part[ix * piece:(ix + 1) * piece, ic * LANES:(ic + 1) * LANES].astype(BF)
    pl.semaphore_wait(barrier, len(peers) + jnp.where(zl == nzl - 1, 1, 0))

    moves = [
        kept(ysend.at[(xc + k) % nxc], yrecv.at[k], y1s.at[k], y1r.at[k], xc_peer(k)) for k in range(1, nxc)
    ]
    load_b.wait()
    for c0 in range(SLAB, WIDTH, 256):
        c1 = min(c0 + 256, WIDTH)
        got = jnp.dot(x_buf[...], fac_buf[:, c0:c1], preferred_element_type=F32) * vee[:, c0:c1]
        inner[:, c0:c1] = got.astype(BF)
    core_move = kept(inner, other, core_sem.at[0], core_sem.at[1], at(zh, y, zl, x * nc + 1 - core))
    total = ysend[xc].astype(F32)
    for k in range(1, nxc):
        moves[k - 1].wait_recv()
        total = total + yrecv[k].astype(F32)
    ymid[...] = total.astype(BF)
    moves2 = [kept(ymid, yzrecv.at[k], y2s.at[k], y2r.at[k], z_peer(k)) for k in range(1, nzl)]
    total = ymid[...].astype(F32)
    for k in range(1, nzl):
        moves2[k - 1].wait_recv()
        total = total + yzrecv[k].astype(F32)
    yfull[xc] = total.astype(BF)
    moves3 = [
        kept(yfull.at[xc], yfull.at[xc], y3s.at[k], y3r.at[k], xc_peer(k)) for k in range(1, nxc)
    ]

    core_move.wait_recv()
    core_sign = (1 - 2 * core).astype(F32)
    other[...] = (other[...].astype(F32) + inner[...].astype(F32) * core_sign).astype(BF)
    for move in moves3:
        move.wait_recv()

    @pl.when(zl == nzl - 1)
    def _():
        pl.semaphore_signal(group_sem, inc=1, device_id=at(1 - zh, y, 0, xc), device_id_type=MESH)

    for half in range(2):
        left = jnp.concatenate([yfull[ix * 2 + half] for ix in range(nx)], axis=0)
        for c0 in range(0, WIDTH, 256):
            c1 = min(c0 + 256, WIDTH)
            got = lax.dot_general(
                left, other[:, c0:c1], (((0,), (0,)), ((), ())), preferred_element_type=F32
            ).astype(BF)
            for iy in range(ny):
                for j in range((c1 - c0) // LANES):
                    gp[iy, c0 // LANES + j, half] = got[iy * rows:(iy + 1) * rows, j * LANES:(j + 1) * LANES]

    chunks = [(NT * m // CHUNKS, NT * (m + 1) // CHUNKS) for m in range(CHUNKS)]
    ways = (1, -1)
    aggs, halves, nears, twos = {}, {}, {}, {}

    def index(kind, way, m):
        return (kind * 2 + (way + 1) // 2) * CHUNKS + m

    def block(to, m):
        lo, hi = chunks[m]
        return gp.at[(y + to + ny) % ny, pl.ds(lo, hi - lo)]

    def slot(ref, way, m):
        lo, hi = chunks[m]
        return ref.at[(way + 1) // 2, pl.ds(lo, hi - lo)]

    def y_send(kind, src, ref, way, m, to):
        n = index(kind, way, m)
        return kept(src, slot(ref, way, m), rss.at[n], rsr.at[n], y_peer(to))

    for m in range(CHUNKS):
        lo, hi = chunks[m]
        for way in ways:
            n = index(1, way, m)
            side = (way + 1) // 2
            halves[way, m] = kept(
                gp.at[(y + ny // 2) % ny, pl.ds(lo, hi - lo), side], slot(rs_half, way, m),
                rss.at[n], rsr.at[n], y_peer(2 * way),
            )
        for way in ways:
            aggs[way, m] = y_send(0, block(3 * way, m), rs_agg, way, m, way)
    for m in range(CHUNKS):
        for way in ways:
            nears[way, m] = y_send(2, block(way, m), rs_near, way, m, way)
    for m in range(CHUNKS):
        lo, hi = chunks[m]
        for way in ways:
            side = (way + 1) // 2
            aggs[way, m].wait_recv()
            halves[way, m].wait_recv()
            for h in range(2):
                total = block(2 * way, m)[:, h].astype(F32) + rs_agg[side, lo:hi, h].astype(F32)
                if h == side:
                    total = total + rs_half[side, lo:hi].astype(F32)
                agg[side, lo:hi, h] = total.astype(BF)
            twos[way, m] = y_send(3, slot(agg, way, m), rs_two, way, m, 2 * way)

    @pl.when(zl == 0)
    def _():
        pl.semaphore_wait(group_sem, 1)
        for k in range(1, nzl):
            pl.semaphore_signal(group_sem, inc=1, device_id=z_peer(k), device_id_type=MESH)

    @pl.when(zl != 0)
    def _():
        pl.semaphore_wait(group_sem, 1)

    for m in range(CHUNKS):
        lo, hi = chunks[m]
        for way in ways:
            nears[way, m].wait_recv()
            twos[way, m].wait_recv()
        for h in range(2):
            total = block(0, m)[:, h].astype(F32)
            for side in range(2):
                total = total + rs_near[side, lo:hi, h].astype(F32) + rs_two[side, lo:hi, h].astype(F32)
            pbuf[h, lo:hi] = total.astype(BF)

    hops = [(a, k) for a in range(2) for k in range(nq) if (a, k) != (0, 0)]

    def mix_move(a, k):
        far = (q + k) % nq
        return pltpu.make_async_remote_copy(
            src_ref=pbuf.at[(zh + a) % 2, far], dst_ref=mbuf.at[zh * nq + q],
            send_sem=ms, recv_sem=mr, device_id=q_peer(a, k), device_id_type=MESH,
        )

    for a, k in hops:
        @pl.when((q + k) % nq < NT)
        def _():
            mix_move(a, k).start()

    def back_move(k):
        return pltpu.make_async_remote_copy(
            src_ref=wbuf.at[(q + k) % nq], dst_ref=obuf.at[q],
            send_sem=bs, recv_sem=br, device_id=q_peer(0, k), device_id_type=MESH,
        )

    def drain(ref, count, sem):
        part = ref.at[pl.ds(0, count)]
        pltpu.make_async_copy(part, part, sem).wait()

    @pl.when(q < NT)
    def _():
        mbuf[zh * nq + q] = pbuf[zh, q]
        drain(mbuf, 2 * nq - 1, mr)
        mixed = butterfly([mbuf[l].astype(F32) + mbuf[nq + l].astype(F32) for l in range(nq)])
        for l in range(nq):
            wbuf[l] = mixed[l].astype(BF)
        for k in range(1, nq):
            back_move(k).start()
        obuf[q] = wbuf[q]
        drain(obuf, NT - 1, br)
        drain(wbuf, nq - 1, bs)
        drain(mbuf, 2 * NT - 1, ms)

    @pl.when(q >= NT)
    def _():
        drain(obuf, NT, br)
        drain(mbuf, 2 * NT, ms)

    for j in range(NT):
        out_ref[:, j * LANES:(j + 1) * LANES] = obuf[j].astype(F32)
    for move in sent:
        move.wait_send()


def shards(dims, activations, sign_bits, factor_bits):
    ny, nzl, nx, nc = dims
    nxc = nx * nc
    nq = nzl * nx
    rows = SLAB // (2 * ny)
    tokens = activations.shape[0]
    piece = tokens // nx
    dma = pltpu.SemaphoreType.DMA
    vm = pltpu.VMEM
    gram = pl.pallas_call(
        functools.partial(kernel, dims),
        out_shape=jax.ShapeDtypeStruct((rows, WIDTH), F32),
        in_specs=[
            pl.BlockSpec(memory_space=pl.ANY),
            pl.BlockSpec(memory_space=pltpu.VMEM),
            pl.BlockSpec(memory_space=pl.ANY),
            pl.BlockSpec(memory_space=pl.ANY),
        ],
        out_specs=pl.BlockSpec(memory_space=pltpu.VMEM),
        scratch_shapes=[
            vm((tokens, WIDTH), BF),
            vm((WIDTH, WIDTH), BF),
            vm((tokens, WIDTH), BF),
            vm((tokens, WIDTH), BF),
            pltpu.SMEM((KF,), jnp.int32),
            vm((nxc, piece, LANES), BF),
            vm((nxc, piece, LANES), BF),
            vm((piece, LANES), BF),
            vm((nzl, piece, LANES), BF),
            vm((nxc, piece, LANES), BF),
            vm((ny, NT, 2, rows, LANES), BF),
            vm((2, NT, 2, rows, LANES), BF),
            vm((2, NT, rows, LANES), BF),
            vm((2, NT, 2, rows, LANES), BF),
            vm((2, NT, 2, rows, LANES), BF),
            vm((2, NT, 2, rows, LANES), BF),
            vm((2, NT, rows, LANES), BF),
            vm((2 * nq, rows, LANES), BF),
            vm((nq, rows, LANES), BF),
            vm((NT, rows, LANES), BF),
            dma((4,)),
            dma((2,)),
            dma((nxc,)), dma((nxc,)),
            dma((nzl,)), dma((nzl,)),
            dma((nxc,)), dma((nxc,)),
            dma((8 * CHUNKS,)), dma((8 * CHUNKS,)),
            dma, dma,
            dma, dma,
            pltpu.SemaphoreType.REGULAR,
        ],
        compiler_params=pltpu.CompilerParams(
            collective_id=0, has_side_effects=True, vmem_limit_bytes=VMEM_LIMIT
        ),
    )(activations, sign_bits, factor_bits, jnp.asarray(small_factor()))
    row = lax.axis_index("dp") * rows + lax.broadcasted_iota(jnp.int32, gram.shape, 0)
    col = lax.axis_index("tile") * WIDTH + lax.broadcasted_iota(jnp.int32, gram.shape, 1)
    keep = col // LANES >= row // LANES
    all_tokens = tokens * 2 * ny
    return jnp.where(keep, gram * (2.0 / all_tokens / HAD), 0.0)


def solution(mesh, dims=(8, 4, 4, 2)):
    return jax.shard_map(
        functools.partial(shards, dims),
        mesh=mesh,
        in_specs=(P("dp", "tile"), P("tile"), P()),
        out_specs=P("dp", "tile"),
        check_vma=False,
    )
```

time: 62.4 us -> 54.3 us (0.87)
  the two profiles are of different devices: /device:TPU:1 before, /device:TPU:6 now
where the time goes in v2:
time: 54.3 us; the launch traced here: 53.9 us
  Pallas kernels  52.2 us (96%)
  other arithmetic  1.67 us (3%)
    pallas_call x1, Pallas kernels, shards(): pl.pallas_call(functools.partial(kernel, dims), out_shape=jax.ShapeDtypeS...  52.2 us
    select_n x1, other arithmetic, shards(): return jnp.where(keep, gram * (2.0 / all_tokens / HAD), 0.0)  1.62 us

profile of v2, /device:TPU:6, one launch (start us, length us, event | category | flops | bytes accessed | tf_op | source)
XLA Modules:
  0.0 53.9 jit_solution(1515855812069093213)
XLA Ops:
  0.1 52.2 %shard_map.46 = f32[16,1664]{1,0:T(8,128)} custom-call(bf16[192,1664]{1,0:T(8,128)(2,1)} %act_hbm.1, s32[1664]{0:T(1024)} %sign_ref.1, s32[13]{0:T(128)} %bits_hbm.1, bf16[1664,1664]{1,0:T(8,128)(2,1)} %constant.50.clone.fac_hbm), custom_call_target="tpu_custom_call" | custom-call | tf_op jit(solution)/shard_map/pallas_call | solution.py:307
  52.3 1.6 %multiply_select_fusion = f32[16,1664]{1,0:T(8,128)} fusion(f32[16,1664]{1,0:T(8,128)} %shard_map.46, s32[16]{0:T(128)S(1)} %get-tuple-element.5, s32[16]{0:T(128)S(1)} %get-tuple-element.6, s32[1664]{0:T(1024)S(1)} %get-tuple-element.7, s32[1664]{0:T(1024)S(1)} %get-tuple-element.8, pred[16]{0:T(512)(128)(4,1)S(1)} %compare_and_fusion, ...), kind=kLoop, calls=%fused_computation | loop fusion | flops 133120 | bytes 228112 | tf_op jit(solution)/shard_map/jit(_where)/select_n | solution.py:356
  (4 shorter events, 0.1 us)

commit v3 on v2

--- a/solution.py
+++ b/solution.py
@@ -16,7 +16,11 @@
 HAD = 4096
 LANES = 128
 NT = WIDTH // LANES
-CHUNKS = 3
+ORDER = (10, 6, 14, 9, 11, 5, 7, 13, 15, 2, 8, 1, 3, 4, 12)
+CUTS = (0, 4, 8, 13)
+CHUNKS = len(CUTS) - 1
+THREE = (True, True, False)
+SPLIT = 1280
 VMEM_LIMIT = 60 * 1024 * 1024
 MESH = pl.DeviceIdType.MESH
 BF = jnp.bfloat16
@@ -48,10 +52,10 @@
 
 def kernel(
     dims,
-    act_hbm, sign_ref, bits_hbm, fac_hbm,
+    act_hbm, sign_hbm, bits_hbm, fac_hbm,
     out_ref,
-    x_buf, fac_buf, inner, other, bits_ref, ysend, yrecv, ymid, yzrecv, yfull,
-    gp, rs_agg, rs_half, rs_near, rs_two, agg, pbuf, mbuf, wbuf, obuf,
+    x_buf, fac_buf, inner, other, sign_ref, bits_ref, ysend, yrecv, ymid, yzrecv, yfull,
+    gp, rs_agg, rs_half, rs_near, rs_two, agg, pbuf, mbuf, wbuf,
     load_sem, core_sem, y1s, y1r, y2s, y2r, y3s, y3r, rss, rsr, ms, mr, bs, br, group_sem,
 ):
     ny, nzl, nx, nc = dims
@@ -65,6 +69,7 @@
     zl, xc = tile // nxc, tile % nxc
     x, core = xc // nc, xc % nc
     q = zl * nx + x
+    mine = (q + nq // 2 * core) % nq
     sent = []
 
     def at(zh_, y_, zl_, xc_):
@@ -79,9 +84,9 @@
     def y_peer(k):
         return at(zh, (y + k + ny) % ny, zl, xc)
 
-    def q_peer(a, k):
+    def q_peer(k):
         far = (q + k) % nq
-        return at((zh + a) % 2, y, far // nx, far % nx * nc + core)
+        return at(zh, y, far // nx, far % nx * nc + core)
 
     def remote(src, dst, send, recv, peer):
         copy = pltpu.make_async_remote_copy(
@@ -94,15 +99,22 @@
         sent.append(remote(*args))
         return sent[-1]
 
+    def settle():
+        for copy in sent:
+            copy.wait_send()
+        sent.clear()
+
     load_bits = pltpu.make_async_copy(bits_hbm, bits_ref, load_sem.at[3])
     load_x = pltpu.make_async_copy(act_hbm, x_buf, load_sem.at[0])
     load_a = pltpu.make_async_copy(fac_hbm.at[:, pl.ds(0, SLAB)], fac_buf.at[:, pl.ds(0, SLAB)], load_sem.at[1])
     load_b = pltpu.make_async_copy(
         fac_hbm.at[:, pl.ds(SLAB, WIDTH - SLAB)], fac_buf.at[:, pl.ds(SLAB, WIDTH - SLAB)], load_sem.at[2]
     )
-    load_bits.start()
+    load_sign = pltpu.make_async_copy(sign_hbm, sign_ref, load_sem.at[4])
     load_x.start()
     load_a.start()
+    load_sign.start()
+    load_bits.start()
     load_b.start()
 
     barrier = pltpu.get_barrier_semaphore()
@@ -117,6 +129,7 @@
 
     col = lax.broadcasted_iota(jnp.int32, (1, WIDTH), 1)
     b_of = col - KF * ((col * 20165) >> 18)
+    load_sign.wait()
     load_bits.wait()
     vee = jnp.zeros((1, WIDTH), F32)
     for b in range(KF):
@@ -134,21 +147,40 @@
             ysend[ix * 2 + ic] = part[ix * piece:(ix + 1) * piece, ic * LANES:(ic + 1) * LANES].astype(BF)
     pl.semaphore_wait(barrier, len(peers) + jnp.where(zl == nzl - 1, 1, 0))
 
+    def more_inner(first, last):
+        for c0 in range(first, last, 256):
+            c1 = min(c0 + 256, last)
+            got = jnp.dot(x_buf[...], fac_buf[:, c0:c1], preferred_element_type=F32) * vee[:, c0:c1]
+            inner[:, c0:c1] = got.astype(BF)
+
+    def swap_cores(n, first, last):
+        part = pl.ds(first, last - first)
+        return kept(
+            inner.at[:, part], other.at[:, part], core_sem.at[n], core_sem.at[2 + n], at(zh, y, zl, x * nc + 1 - core)
+        )
+
+    def mix_cores(n, first, last):
+        core_moves[n].wait_recv()
+        sign = (1 - 2 * core).astype(F32)
+        other[:, first:last] = (
+            other[:, first:last].astype(F32) + inner[:, first:last].astype(F32) * sign
+        ).astype(BF)
+
     moves = [
         kept(ysend.at[(xc + k) % nxc], yrecv.at[k], y1s.at[k], y1r.at[k], xc_peer(k)) for k in range(1, nxc)
     ]
     load_b.wait()
-    for c0 in range(SLAB, WIDTH, 256):
-        c1 = min(c0 + 256, WIDTH)
-        got = jnp.dot(x_buf[...], fac_buf[:, c0:c1], preferred_element_type=F32) * vee[:, c0:c1]
-        inner[:, c0:c1] = got.astype(BF)
-    core_move = kept(inner, other, core_sem.at[0], core_sem.at[1], at(zh, y, zl, x * nc + 1 - core))
+    more_inner(SLAB, SPLIT)
+    core_moves = [swap_cores(0, 0, SPLIT)]
     total = ysend[xc].astype(F32)
     for k in range(1, nxc):
         moves[k - 1].wait_recv()
         total = total + yrecv[k].astype(F32)
     ymid[...] = total.astype(BF)
     moves2 = [kept(ymid, yzrecv.at[k], y2s.at[k], y2r.at[k], z_peer(k)) for k in range(1, nzl)]
+    more_inner(SPLIT, WIDTH)
+    core_moves.append(swap_cores(1, SPLIT, WIDTH))
+    mix_cores(0, 0, SPLIT)
     total = ymid[...].astype(F32)
     for k in range(1, nzl):
         moves2[k - 1].wait_recv()
@@ -158,9 +190,7 @@
         kept(yfull.at[xc], yfull.at[xc], y3s.at[k], y3r.at[k], xc_peer(k)) for k in range(1, nxc)
     ]
 
-    core_move.wait_recv()
-    core_sign = (1 - 2 * core).astype(F32)
-    other[...] = (other[...].astype(F32) + inner[...].astype(F32) * core_sign).astype(BF)
+    mix_cores(1, SPLIT, WIDTH)
     for move in moves3:
         move.wait_recv()
 
@@ -168,18 +198,18 @@
     def _():
         pl.semaphore_signal(group_sem, inc=1, device_id=at(1 - zh, y, 0, xc), device_id_type=MESH)
 
-    for half in range(2):
-        left = jnp.concatenate([yfull[ix * 2 + half] for ix in range(nx)], axis=0)
-        for c0 in range(0, WIDTH, 256):
-            c1 = min(c0 + 256, WIDTH)
-            got = lax.dot_general(
-                left, other[:, c0:c1], (((0,), (0,)), ((), ())), preferred_element_type=F32
-            ).astype(BF)
-            for iy in range(ny):
-                for j in range((c1 - c0) // LANES):
-                    gp[iy, c0 // LANES + j, half] = got[iy * rows:(iy + 1) * rows, j * LANES:(j + 1) * LANES]
-
-    chunks = [(NT * m // CHUNKS, NT * (m + 1) // CHUNKS) for m in range(CHUNKS)]
+    lefts = [jnp.concatenate([yfull[ix * 2 + half] for ix in range(nx)], axis=0).T for half in range(2)]
+
+    def gram_terms(first, last):
+        for c0 in range(first * LANES, last * LANES, 256):
+            c1 = min(c0 + 256, last * LANES)
+            for half in range(2):
+                got = jnp.dot(lefts[half], other[:, c0:c1], preferred_element_type=F32).astype(BF)
+                for iy in range(ny):
+                    for j in range((c1 - c0) // LANES):
+                        gp[iy, c0 // LANES + j, half] = got[iy * rows:(iy + 1) * rows, j * LANES:(j + 1) * LANES]
+
+    chunks = list(zip(CUTS[:-1], CUTS[1:]))
     ways = (1, -1)
     aggs, halves, nears, twos = {}, {}, {}, {}
 
@@ -200,6 +230,7 @@
 
     for m in range(CHUNKS):
         lo, hi = chunks[m]
+        gram_terms(lo, hi)
         for way in ways:
             n = index(1, way, m)
             side = (way + 1) // 2
@@ -210,8 +241,9 @@
         for way in ways:
             aggs[way, m] = y_send(0, block(3 * way, m), rs_agg, way, m, way)
     for m in range(CHUNKS):
-        for way in ways:
-            nears[way, m] = y_send(2, block(way, m), rs_near, way, m, way)
+        if not THREE[m]:
+            for way in ways:
+                nears[way, m] = y_send(2, block(way, m), rs_near, way, m, way)
     for m in range(CHUNKS):
         lo, hi = chunks[m]
         for way in ways:
@@ -223,7 +255,15 @@
                 if h == side:
                     total = total + rs_half[side, lo:hi].astype(F32)
                 agg[side, lo:hi, h] = total.astype(BF)
-            twos[way, m] = y_send(3, slot(agg, way, m), rs_two, way, m, 2 * way)
+            twos[way, m] = y_send(3, slot(agg, way, m), rs_two, way, m, way if THREE[m] else 2 * way)
+    for m in range(CHUNKS):
+        if THREE[m]:
+            lo, hi = chunks[m]
+            for way in ways:
+                side = (way + 1) // 2
+                twos[way, m].wait_recv()
+                rs_two[side, lo:hi] = (rs_two[side, lo:hi].astype(F32) + block(way, m)[...].astype(F32)).astype(BF)
+                nears[way, m] = y_send(2, slot(rs_two, way, m), rs_near, way, m, way)
 
     @pl.when(zl == 0)
     def _():
@@ -234,65 +274,68 @@
     @pl.when(zl != 0)
     def _():
         pl.semaphore_wait(group_sem, 1)
+
+    def mix_move(a, p):
+        return pltpu.make_async_remote_copy(
+            src_ref=pbuf.at[(zh + a) % 2, p], dst_ref=mbuf.at[zh * nq + q], send_sem=ms, recv_sem=mr,
+            device_id=at((zh + a) % 2, y, (p // nx + nzl // 2 * core) % nzl, p % nx * nc + core),
+            device_id_type=MESH,
+        )
 
     for m in range(CHUNKS):
         lo, hi = chunks[m]
         for way in ways:
             nears[way, m].wait_recv()
-            twos[way, m].wait_recv()
+            if not THREE[m]:
+                twos[way, m].wait_recv()
         for h in range(2):
             total = block(0, m)[:, h].astype(F32)
             for side in range(2):
-                total = total + rs_near[side, lo:hi, h].astype(F32) + rs_two[side, lo:hi, h].astype(F32)
+                total = total + rs_near[side, lo:hi, h].astype(F32)
+                if not THREE[m]:
+                    total = total + rs_two[side, lo:hi, h].astype(F32)
             pbuf[h, lo:hi] = total.astype(BF)
-
-    hops = [(a, k) for a in range(2) for k in range(nq) if (a, k) != (0, 0)]
-
-    def mix_move(a, k):
-        far = (q + k) % nq
-        return pltpu.make_async_remote_copy(
-            src_ref=pbuf.at[(zh + a) % 2, far], dst_ref=mbuf.at[zh * nq + q],
-            send_sem=ms, recv_sem=mr, device_id=q_peer(a, k), device_id_type=MESH,
-        )
-
-    for a, k in hops:
-        @pl.when((q + k) % nq < NT)
-        def _():
-            mix_move(a, k).start()
+        for p in range(lo, hi):
+            mix_move(1, p).start()
+        for p in range(lo, hi):
+            @pl.when(mine != p)
+            def _():
+                mix_move(0, p).start()
+
+    settle()
 
     def back_move(k):
         return pltpu.make_async_remote_copy(
-            src_ref=wbuf.at[(q + k) % nq], dst_ref=obuf.at[q],
-            send_sem=bs, recv_sem=br, device_id=q_peer(0, k), device_id_type=MESH,
+            src_ref=wbuf.at[(q + k) % nq], dst_ref=out_ref.at[:, pl.ds(pl.multiple_of(mine * LANES, LANES), LANES)],
+            send_sem=bs, recv_sem=br, device_id=q_peer(k), device_id_type=MESH,
         )
 
     def drain(ref, count, sem):
         part = ref.at[pl.ds(0, count)]
         pltpu.make_async_copy(part, part, sem).wait()
 
-    @pl.when(q < NT)
-    def _():
-        mbuf[zh * nq + q] = pbuf[zh, q]
+    @pl.when(mine < NT)
+    def _():
+        mbuf[zh * nq + q] = pbuf[zh, mine]
         drain(mbuf, 2 * nq - 1, mr)
         mixed = butterfly([mbuf[l].astype(F32) + mbuf[nq + l].astype(F32) for l in range(nq)])
         for l in range(nq):
             wbuf[l] = mixed[l].astype(BF)
-        for k in range(1, nq):
+        for k in ORDER:
             back_move(k).start()
-        obuf[q] = wbuf[q]
-        drain(obuf, NT - 1, br)
+        own = pltpu.make_async_copy(
+            wbuf.at[q], out_ref.at[:, pl.ds(pl.multiple_of(mine * LANES, LANES), LANES)], load_sem.at[5]
+        )
+        own.start()
+        drain(mbuf, 2 * NT - 1, ms)
+        own.wait()
+        drain(mbuf, NT - 1, br)
         drain(wbuf, nq - 1, bs)
-        drain(mbuf, 2 * NT - 1, ms)
-
-    @pl.when(q >= NT)
-    def _():
-        drain(obuf, NT, br)
+
+    @pl.when(mine >= NT)
+    def _():
         drain(mbuf, 2 * NT, ms)
-
-    for j in range(NT):
-        out_ref[:, j * LANES:(j + 1) * LANES] = obuf[j].astype(F32)
-    for move in sent:
-        move.wait_send()
+        drain(mbuf, NT, br)
 
 
 def shards(dims, activations, sign_bits, factor_bits):
@@ -306,19 +349,20 @@
     vm = pltpu.VMEM
     gram = pl.pallas_call(
         functools.partial(kernel, dims),
-        out_shape=jax.ShapeDtypeStruct((rows, WIDTH), F32),
+        out_shape=jax.ShapeDtypeStruct((rows, WIDTH), BF),
         in_specs=[
             pl.BlockSpec(memory_space=pl.ANY),
-            pl.BlockSpec(memory_space=pltpu.VMEM),
+            pl.BlockSpec(memory_space=pl.ANY),
             pl.BlockSpec(memory_space=pl.ANY),
             pl.BlockSpec(memory_space=pl.ANY),
         ],
-        out_specs=pl.BlockSpec(memory_space=pltpu.VMEM),
+        out_specs=pl.BlockSpec(memory_space=pl.ANY),
         scratch_shapes=[
             vm((tokens, WIDTH), BF),
             vm((WIDTH, WIDTH), BF),
             vm((tokens, WIDTH), BF),
             vm((tokens, WIDTH), BF),
+            vm((WIDTH,), jnp.int32),
             pltpu.SMEM((KF,), jnp.int32),
             vm((nxc, piece, LANES), BF),
             vm((nxc, piece, LANES), BF),
@@ -334,9 +378,8 @@
             vm((2, NT, rows, LANES), BF),
             vm((2 * nq, rows, LANES), BF),
             vm((nq, rows, LANES), BF),
-            vm((NT, rows, LANES), BF),
+            dma((6,)),
             dma((4,)),
-            dma((2,)),
             dma((nxc,)), dma((nxc,)),
             dma((nzl,)), dma((nzl,)),
             dma((nxc,)), dma((nxc,)),
@@ -353,7 +396,7 @@
     col = lax.axis_index("tile") * WIDTH + lax.broadcasted_iota(jnp.int32, gram.shape, 1)
     keep = col // LANES >= row // LANES
     all_tokens = tokens * 2 * ny
-    return jnp.where(keep, gram * (2.0 / all_tokens / HAD), 0.0)
+    return jnp.where(keep, gram.astype(F32) * (2.0 / all_tokens / HAD), 0.0)
 
 
 def solution(mesh, dims=(8, 4, 4, 2)):

time: 54.3 us -> 50.6 us (0.932)
  Pallas kernels: 52.2 us -> 48.7 us
    pallas_call x1, Pallas kernels: 52.2 us -> 48.7 us  [shards(): pl.pallas_call(functools.partial(kernel, dims), out_shape=jax.ShapeDtypeS...]
where the time goes in v3:
time: 50.6 us; the launch traced here: 50.3 us
  Pallas kernels  48.7 us (96%)
  other arithmetic  1.59 us (3%)
    pallas_call x1, Pallas kernels, shards(): pl.pallas_call(functools.partial(kernel, dims), out_shape=jax.ShapeDtypeS...  48.7 us
    select_n x1, other arithmetic, shards(): return jnp.where(keep, gram.astype(F32) * (2.0 / all_tokens / HAD), 0.0)  1.53 us

profile of v3, /device:TPU:6, one launch (start us, length us, event | category | flops | bytes accessed | tf_op | source)
XLA Modules:
  0.0 50.3 jit_solution(16070532364987679342)
XLA Ops:
  0.1 48.7 %shard_map.46 = bf16[16,1664]{1,0:T(8,128)(2,1)} custom-call(bf16[192,1664]{1,0:T(8,128)(2,1)} %act_hbm.1, s32[1664]{0:T(1024)} %sign_hbm.1, s32[13]{0:T(128)} %bits_hbm.1, bf16[1664,1664]{1,0:T(8,128)(2,1)} %constant.50.clone.fac_hbm), custom_call_target="tpu_custom_call" | custom-call | tf_op jit(solution)/shard_map/pallas_call | solution.py:350
  48.8 1.5 %multiply_select_fusion = f32[16,1664]{1,0:T(8,128)} fusion(bf16[16,1664]{1,0:T(8,128)(2,1)} %shard_map.46, s32[16]{0:T(128)S(1)} %get-tuple-element.5, s32[16]{0:T(128)S(1)} %get-tuple-element.6, s32[1664]{0:T(1024)S(1)} %get-tuple-element.7, s32[1664]{0:T(1024)S(1)} %get-tuple-element.8, pred[16]{0:T(512)(128)(4,1)S(1)} %compare_and_fusion, ...), kind=kLoop, calls=%fused_computation | loop fusion | flops 159744 | bytes 174864 | tf_op jit(solution)/shard_map/jit(_where)/select_n | solution.py:399
  (4 shorter events, 0.1 us)

commit v4 on v3

--- a/solution.py
+++ b/solution.py
@@ -16,7 +16,8 @@
 HAD = 4096
 LANES = 128
 NT = WIDTH // LANES
-ORDER = (10, 6, 14, 9, 11, 5, 7, 13, 15, 2, 8, 1, 3, 4, 12)
+NU = (NT + 1) // 2
+BACK = ((2, 2), (1, 2), (3, 2), (2, 1), (2, 3), (1, 1), (1, 3), (3, 1), (3, 3), (2, 0), (0, 2), (1, 0), (3, 0), (0, 1), (0, 3))
 CUTS = (0, 4, 8, 13)
 CHUNKS = len(CUTS) - 1
 THREE = (True, True, False)
@@ -69,7 +70,9 @@
     zl, xc = tile // nxc, tile % nxc
     x, core = xc // nc, xc % nc
     q = zl * nx + x
-    mine = (q + nq // 2 * core) % nq
+    middle = (zl + 1) // 2 % 2
+    mine = ((zl - 1) * nx + x + nx * core + 2 * nx) % (2 * nx)
+    owner_here = middle * jnp.where(mine < NU, 1, 0) == 1
     sent = []
 
     def at(zh_, y_, zl_, xc_):
@@ -275,10 +278,11 @@
     def _():
         pl.semaphore_wait(group_sem, 1)
 
-    def mix_move(a, p):
+    def mix_move(a, u):
+        spot = u + nx * core
         return pltpu.make_async_remote_copy(
-            src_ref=pbuf.at[(zh + a) % 2, p], dst_ref=mbuf.at[zh * nq + q], send_sem=ms, recv_sem=mr,
-            device_id=at((zh + a) % 2, y, (p // nx + nzl // 2 * core) % nzl, p % nx * nc + core),
+            src_ref=pbuf.at[(zh + a) % 2, pl.ds(2 * u, 2)], dst_ref=mbuf.at[zh * nq + q], send_sem=ms, recv_sem=mr,
+            device_id=at((zh + a) % 2, y, 1 + spot // nx % 2, spot % nx * nc + core),
             device_id_type=MESH,
         )
 
@@ -295,47 +299,53 @@
                 if not THREE[m]:
                     total = total + rs_two[side, lo:hi, h].astype(F32)
             pbuf[h, lo:hi] = total.astype(BF)
-        for p in range(lo, hi):
-            mix_move(1, p).start()
-        for p in range(lo, hi):
-            @pl.when(mine != p)
+            if hi == NT:
+                for j in range(NT, 2 * NU):
+                    pbuf[h, j] = jnp.zeros((rows, LANES), BF)
+        for u in range(lo // 2, (hi + 1) // 2):
+            mix_move(1, u).start()
+        for u in range(lo // 2, (hi + 1) // 2):
+            @pl.when(jnp.logical_not(jnp.logical_and(owner_here, mine == u)))
             def _():
-                mix_move(0, p).start()
+                mix_move(0, u).start()
 
     settle()
 
-    def back_move(k):
+    def columns(u):
+        return pl.ds(pl.multiple_of(u * 2 * LANES, 2 * LANES), 2 * LANES)
+
+    def back_move(dz, dx):
+        far_z, far_x = (zl + dz) % nzl, (x + dx) % nx
         return pltpu.make_async_remote_copy(
-            src_ref=wbuf.at[(q + k) % nq], dst_ref=out_ref.at[:, pl.ds(pl.multiple_of(mine * LANES, LANES), LANES)],
-            send_sem=bs, recv_sem=br, device_id=q_peer(k), device_id_type=MESH,
+            src_ref=wbuf.at[far_z * nx + far_x], dst_ref=out_ref.at[:, columns(mine)],
+            send_sem=bs, recv_sem=br, device_id=at(zh, y, far_z, far_x * nc + core), device_id_type=MESH,
         )
 
     def drain(ref, count, sem):
         part = ref.at[pl.ds(0, count)]
         pltpu.make_async_copy(part, part, sem).wait()
 
-    @pl.when(mine < NT)
-    def _():
-        mbuf[zh * nq + q] = pbuf[zh, mine]
+    @pl.when(owner_here)
+    def _():
+        mbuf[zh * nq + q] = pbuf[zh, pl.ds(2 * mine, 2)]
         drain(mbuf, 2 * nq - 1, mr)
         mixed = butterfly([mbuf[l].astype(F32) + mbuf[nq + l].astype(F32) for l in range(nq)])
         for l in range(nq):
-            wbuf[l] = mixed[l].astype(BF)
-        for k in ORDER:
-            back_move(k).start()
-        own = pltpu.make_async_copy(
-            wbuf.at[q], out_ref.at[:, pl.ds(pl.multiple_of(mine * LANES, LANES), LANES)], load_sem.at[5]
-        )
+            for j in range(2):
+                wbuf[l, :, j * LANES:(j + 1) * LANES] = mixed[l][j].astype(BF)
+        for dz, dx in BACK:
+            back_move(dz, dx).start()
+        own = pltpu.make_async_copy(wbuf.at[q], out_ref.at[:, columns(mine)], load_sem.at[5])
         own.start()
-        drain(mbuf, 2 * NT - 1, ms)
+        drain(mbuf, 2 * NU - 1, ms)
         own.wait()
-        drain(mbuf, NT - 1, br)
+        drain(mbuf, NU - 1, br)
         drain(wbuf, nq - 1, bs)
 
-    @pl.when(mine >= NT)
-    def _():
-        drain(mbuf, 2 * NT, ms)
-        drain(mbuf, NT, br)
+    @pl.when(jnp.logical_not(owner_here))
+    def _():
+        drain(mbuf, 2 * NU, ms)
+        drain(mbuf, NU, br)
 
 
 def shards(dims, activations, sign_bits, factor_bits):
@@ -349,7 +359,7 @@
     vm = pltpu.VMEM
     gram = pl.pallas_call(
         functools.partial(kernel, dims),
-        out_shape=jax.ShapeDtypeStruct((rows, WIDTH), BF),
+        out_shape=jax.ShapeDtypeStruct((rows, 2 * NU * LANES), BF),
         in_specs=[
             pl.BlockSpec(memory_space=pl.ANY),
             pl.BlockSpec(memory_space=pl.ANY),
@@ -375,9 +385,9 @@
             vm((2, NT, 2, rows, LANES), BF),
             vm((2, NT, 2, rows, LANES), BF),
             vm((2, NT, 2, rows, LANES), BF),
-            vm((2, NT, rows, LANES), BF),
-            vm((2 * nq, rows, LANES), BF),
-            vm((nq, rows, LANES), BF),
+            vm((2, 2 * NU, rows, LANES), BF),
+            vm((2 * nq, 2, rows, LANES), BF),
+            vm((nq, rows, 2 * LANES), BF),
             dma((6,)),
             dma((4,)),
             dma((nxc,)), dma((nxc,)),
@@ -391,7 +401,7 @@
         compiler_params=pltpu.CompilerParams(
             collective_id=0, has_side_effects=True, vmem_limit_bytes=VMEM_LIMIT
         ),
-    )(activations, sign_bits, factor_bits, jnp.asarray(small_factor()))
+    )(activations, sign_bits, factor_bits, jnp.asarray(small_factor()))[:, :WIDTH]
     row = lax.axis_index("dp") * rows + lax.broadcasted_iota(jnp.int32, gram.shape, 0)
     col = lax.axis_index("tile") * WIDTH + lax.broadcasted_iota(jnp.int32, gram.shape, 1)
     keep = col // LANES >= row // LANES

time: 50.6 us -> 50.3 us (level)
  no operation moved by 1% of the time
where the time goes in v4:
time: 50.3 us; the launch traced here: 50 us
  Pallas kernels  48.4 us (96%)
  other arithmetic  1.59 us (3%)
    pallas_call x1, Pallas kernels, shards(): pl.pallas_call(functools.partial(kernel, dims), out_shape=jax.ShapeDtypeS...  48.4 us
    select_n x1, other arithmetic, shards(): return jnp.where(keep, gram.astype(F32) * (2.0 / all_tokens / HAD), 0.0)  1.53 us

profile of v4, /device:TPU:6, one launch (start us, length us, event | category | flops | bytes accessed | tf_op | source)
XLA Modules:
  0.0 50.0 jit_solution(14987432235964790106)
XLA Ops:
  0.1 48.4 %shard_map.46 = bf16[16,1792]{1,0:T(8,128)(2,1)} custom-call(bf16[192,1664]{1,0:T(8,128)(2,1)} %act_hbm.1, s32[1664]{0:T(1024)} %sign_hbm.1, s32[13]{0:T(128)} %bits_hbm.1, bf16[1664,1664]{1,0:T(8,128)(2,1)} %constant.50.clone.fac_hbm), custom_call_target="tpu_custom_call" | custom-call | tf_op jit(solution)/shard_map/pallas_call | solution.py:360
  48.5 1.5 %multiply_select_fusion = f32[16,1664]{1,0:T(8,128)} fusion(bf16[16,1792]{1,0:T(8,128)(2,1)} %shard_map.46, s32[16]{0:T(128)S(1)} %get-tuple-element.5, s32[16]{0:T(128)S(1)} %get-tuple-element.6, s32[1664]{0:T(1024)S(1)} %get-tuple-element.7, s32[1664]{0:T(1024)S(1)} %get-tuple-element.8, pred[16]{0:T(512)(128)(4,1)S(1)} %compare_and_fusion, ...), kind=kLoop, calls=%fused_computation | loop fusion | flops 159744 | bytes 174864 | tf_op jit(solution)/shard_map/jit(_where)/select_n | solution.py:409
  (4 shorter events, 0.1 us)

commit v5 on v4

--- a/solution.py
+++ b/solution.py
@@ -22,7 +22,7 @@
 CHUNKS = len(CUTS) - 1
 THREE = (True, True, False)
 SPLIT = 1280
-VMEM_LIMIT = 60 * 1024 * 1024
+VMEM_LIMIT = 40 * 1024 * 1024
 MESH = pl.DeviceIdType.MESH
 BF = jnp.bfloat16
 F32 = jnp.float32
@@ -357,6 +357,10 @@
     piece = tokens // nx
     dma = pltpu.SemaphoreType.DMA
     vm = pltpu.VMEM
+    in_hbm = [
+        pltpu.with_memory_space_constraint(array, pltpu.HBM)
+        for array in (activations, sign_bits, factor_bits, jnp.asarray(small_factor()))
+    ]
     gram = pl.pallas_call(
         functools.partial(kernel, dims),
         out_shape=jax.ShapeDtypeStruct((rows, 2 * NU * LANES), BF),
@@ -401,7 +405,7 @@
         compiler_params=pltpu.CompilerParams(
             collective_id=0, has_side_effects=True, vmem_limit_bytes=VMEM_LIMIT
         ),
-    )(activations, sign_bits, factor_bits, jnp.asarray(small_factor()))[:, :WIDTH]
+    )(*in_hbm)[:, :WIDTH]
     row = lax.axis_index("dp") * rows + lax.broadcasted_iota(jnp.int32, gram.shape, 0)
     col = lax.axis_index("tile") * WIDTH + lax.broadcasted_iota(jnp.int32, gram.shape, 1)
     keep = col // LANES >= row // LANES

time: 50.3 us -> 49.3 us (0.980)
  other arithmetic: 1.59 us -> 0.78 us
    select_n x1, other arithmetic: 1.53 us -> 0.72 us  [shards(): return jnp.where(keep, gram.astype(F32) * (2.0 / all_tokens / HAD), 0.0)]
where the time goes in v5:
time: 49.3 us; the launch traced here: 49.1 us
  Pallas kernels  48.3 us (98%)
  other arithmetic  0.78 us (2%)
    pallas_call x1, Pallas kernels, shards(): pl.pallas_call(functools.partial(kernel, dims), out_shape=jax.ShapeDtypeS...  48.3 us

profile of v5, /device:TPU:6, one launch (start us, length us, event | category | flops | bytes accessed | tf_op | source)
XLA Modules:
  0.0 49.1 jit_solution(14091523044099992100)
XLA Ops:
  0.1 48.3 %shard_map.46 = bf16[16,1792]{1,0:T(8,128)(2,1)S(1)} custom-call(bf16[192,1664]{1,0:T(8,128)(2,1)} %act_hbm.1, s32[1664]{0:T(1024)} %sign_hbm.1, s32[13]{0:T(128)} %bits_hbm.1, bf16[1664,1664]{1,0:T(8,128)(2,1)} %constant.50.clone.fac_hbm), custom_call_target="tpu_custom_call" | custom-call | tf_op jit(solution)/shard_map/pallas_call | solution.py:364
  48.4 0.7 %multiply_select_fusion = f32[16,1664]{1,0:T(8,128)} fusion(bf16[16,1792]{1,0:T(8,128)(2,1)S(1)} %shard_map.46, s32[16]{0:T(128)S(1)} %get-tuple-element.5, s32[16]{0:T(128)S(1)} %get-tuple-element.6, s32[1664]{0:T(1024)S(1)} %get-tuple-element.7, s32[1664]{0:T(1024)S(1)} %get-tuple-element.8, pred[16]{0:T(512)(128)(4,1)S(1)} %compare_and_fusion, ...), kind=kLoop, calls=%fused_computation | loop fusion | flops 159744 | bytes 174864 | tf_op jit(solution)/shard_map/jit(_where)/select_n | solution.py:413
  (4 shorter events, 0.1 us)

commit v6 on v5

--- a/solution.py
+++ b/solution.py
@@ -18,6 +18,7 @@
 NT = WIDTH // LANES
 NU = (NT + 1) // 2
 BACK = ((2, 2), (1, 2), (3, 2), (2, 1), (2, 3), (1, 1), (1, 3), (3, 1), (3, 3), (2, 0), (0, 2), (1, 0), (3, 0), (0, 1), (0, 3))
+FAR_FIRST = (4, 3, 5, 2, 6, 7, 1)
 CUTS = (0, 4, 8, 13)
 CHUNKS = len(CUTS) - 1
 THREE = (True, True, False)
@@ -170,14 +171,14 @@
         ).astype(BF)
 
     moves = [
-        kept(ysend.at[(xc + k) % nxc], yrecv.at[k], y1s.at[k], y1r.at[k], xc_peer(k)) for k in range(1, nxc)
+        kept(ysend.at[(xc + k) % nxc], yrecv.at[k], y1s.at[k], y1r.at[k], xc_peer(k)) for k in FAR_FIRST
     ]
     load_b.wait()
     more_inner(SLAB, SPLIT)
     core_moves = [swap_cores(0, 0, SPLIT)]
     total = ysend[xc].astype(F32)
     for k in range(1, nxc):
-        moves[k - 1].wait_recv()
+        moves[FAR_FIRST.index(k)].wait_recv()
         total = total + yrecv[k].astype(F32)
     ymid[...] = total.astype(BF)
     moves2 = [kept(ymid, yzrecv.at[k], y2s.at[k], y2r.at[k], z_peer(k)) for k in range(1, nzl)]
@@ -190,7 +191,7 @@
         total = total + yzrecv[k].astype(F32)
     yfull[xc] = total.astype(BF)
     moves3 = [
-        kept(yfull.at[xc], yfull.at[xc], y3s.at[k], y3r.at[k], xc_peer(k)) for k in range(1, nxc)
+        kept(yfull.at[xc], yfull.at[xc], y3s.at[k], y3r.at[k], xc_peer(k)) for k in FAR_FIRST
     ]
 
     mix_cores(1, SPLIT, WIDTH)
@@ -330,9 +331,13 @@
         mbuf[zh * nq + q] = pbuf[zh, pl.ds(2 * mine, 2)]
         drain(mbuf, 2 * nq - 1, mr)
         mixed = butterfly([mbuf[l].astype(F32) + mbuf[nq + l].astype(F32) for l in range(nq)])
+        below = jnp.logical_and(jnp.logical_and(zh == 1, core == 0), mine == 0)
         for l in range(nq):
             for j in range(2):
-                wbuf[l, :, j * LANES:(j + 1) * LANES] = mixed[l][j].astype(BF)
+                value = mixed[l][j]
+                if (l, j) == (0, 0):
+                    value = value * jnp.where(below, 0.0, 1.0)
+                wbuf[l, :, j * LANES:(j + 1) * LANES] = value.astype(BF)
         for dz, dx in BACK:
             back_move(dz, dx).start()
         own = pltpu.make_async_copy(wbuf.at[q], out_ref.at[:, columns(mine)], load_sem.at[5])
@@ -406,11 +411,7 @@
             collective_id=0, has_side_effects=True, vmem_limit_bytes=VMEM_LIMIT
         ),
     )(*in_hbm)[:, :WIDTH]
-    row = lax.axis_index("dp") * rows + lax.broadcasted_iota(jnp.int32, gram.shape, 0)
-    col = lax.axis_index("tile") * WIDTH + lax.broadcasted_iota(jnp.int32, gram.shape, 1)
-    keep = col // LANES >= row // LANES
-    all_tokens = tokens * 2 * ny
-    return jnp.where(keep, gram.astype(F32) * (2.0 / all_tokens / HAD), 0.0)
+    return gram.astype(F32) * (2.0 / (tokens * 2 * ny) / HAD)
 
 
 def solution(mesh, dims=(8, 4, 4, 2)):

time: 49.3 us -> 48.9 us (level)
    select_n x1 -> x0, other arithmetic: 0.72 us -> none  [shards(): return jnp.where(keep, gram.astype(F32) * (2.0 / all_tokens / HAD), 0.0)]
    mul x0 -> x1, other arithmetic: none -> 0.65 us  [shards(): return gram.astype(F32) * (2.0 / (tokens * 2 * ny) / HAD)]
where the time goes in v6:
time: 48.9 us; the launch traced here: 48.5 us
  Pallas kernels  47.9 us (98%)
  other arithmetic  0.65 us (1%)
    pallas_call x1, Pallas kernels, shards(): pl.pallas_call(functools.partial(kernel, dims), out_shape=jax.ShapeDtypeS...  47.9 us

profile of v6, /device:TPU:6, one launch (start us, length us, event | category | flops | bytes accessed | tf_op | source)
XLA Modules:
  0.0 48.5 jit_solution(4890578135774061075)
XLA Ops:
  0.0 47.9 %shard_map.46 = bf16[16,1792]{1,0:T(8,128)(2,1)S(1)} custom-call(bf16[192,1664]{1,0:T(8,128)(2,1)} %act_hbm.1, s32[1664]{0:T(1024)} %sign_hbm.1, s32[13]{0:T(128)} %bits_hbm.1, bf16[1664,1664]{1,0:T(8,128)(2,1)} %constant.4.clone.fac_hbm), custom_call_target="tpu_custom_call" | custom-call | tf_op jit(solution)/shard_map/pallas_call | solution.py:369
  47.9 0.7 %convert_multiply_fusion = f32[16,1664]{1,0:T(8,128)} fusion(bf16[16,1792]{1,0:T(8,128)(2,1)S(1)} %shard_map.46), kind=kLoop, calls=%fused_computation | loop fusion | flops 53248 | bytes 159744 | tf_op jit(solution)/shard_map/mul | solution.py:414

commit v7 on v6

--- a/solution.py
+++ b/solution.py
@@ -18,6 +18,7 @@
 NT = WIDTH // LANES
 NU = (NT + 1) // 2
 BACK = ((2, 2), (1, 2), (3, 2), (2, 1), (2, 3), (1, 1), (1, 3), (3, 1), (3, 3), (2, 0), (0, 2), (1, 0), (3, 0), (0, 1), (0, 3))
+Z_FAR_FIRST = (2, 1, 3)
 FAR_FIRST = (4, 3, 5, 2, 6, 7, 1)
 CUTS = (0, 4, 8, 13)
 CHUNKS = len(CUTS) - 1
@@ -181,13 +182,13 @@
         moves[FAR_FIRST.index(k)].wait_recv()
         total = total + yrecv[k].astype(F32)
     ymid[...] = total.astype(BF)
-    moves2 = [kept(ymid, yzrecv.at[k], y2s.at[k], y2r.at[k], z_peer(k)) for k in range(1, nzl)]
+    moves2 = [kept(ymid, yzrecv.at[k], y2s.at[k], y2r.at[k], z_peer(k)) for k in Z_FAR_FIRST]
     more_inner(SPLIT, WIDTH)
     core_moves.append(swap_cores(1, SPLIT, WIDTH))
     mix_cores(0, 0, SPLIT)
     total = ymid[...].astype(F32)
     for k in range(1, nzl):
-        moves2[k - 1].wait_recv()
+        moves2[Z_FAR_FIRST.index(k)].wait_recv()
         total = total + yzrecv[k].astype(F32)
     yfull[xc] = total.astype(BF)
     moves3 = [

time: 48.9 us -> 49 us (level)
  no operation moved by 1% of the time
where the time goes in v7:
time: 49 us; the launch traced here: 48.5 us
  Pallas kernels  47.8 us (98%)
  other arithmetic  0.65 us (1%)
    pallas_call x1, Pallas kernels, shards(): pl.pallas_call(functools.partial(kernel, dims), out_shape=jax.ShapeDtypeS...  47.8 us

profile of v7, /device:TPU:6, one launch (start us, length us, event | category | flops | bytes accessed | tf_op | source)
XLA Modules:
  0.0 48.5 jit_solution(6235809507361568362)
XLA Ops:
  0.0 47.8 %shard_map.46 = bf16[16,1792]{1,0:T(8,128)(2,1)S(1)} custom-call(bf16[192,1664]{1,0:T(8,128)(2,1)} %act_hbm.1, s32[1664]{0:T(1024)} %sign_hbm.1, s32[13]{0:T(128)} %bits_hbm.1, bf16[1664,1664]{1,0:T(8,128)(2,1)} %constant.4.clone.fac_hbm), custom_call_target="tpu_custom_call" | custom-call | tf_op jit(solution)/shard_map/pallas_call | solution.py:370
  47.9 0.7 %convert_multiply_fusion = f32[16,1664]{1,0:T(8,128)} fusion(bf16[16,1792]{1,0:T(8,128)(2,1)S(1)} %shard_map.46), kind=kLoop, calls=%fused_computation | loop fusion | flops 53248 | bytes 159744 | tf_op jit(solution)/shard_map/mul | solution.py:415
